TPU v7x, 32 devices: a whole 2x2x4 slice. The times are simulated.
32 devices in a mesh: dp: 8 (over z, core), tensor: 4 (over y, x).
Axes of the slice: x: 2, y: 2, z: 4, core: 2. Of those that a mesh axis runs over, the one named last changes fastest.
Arguments:
- token_ids: int32 [256], P('dp'), may hold values from 0 to 128255, as said below
- hidden_in: bfloat16 [256, 8192], P('dp'), may hold values from -6 to 6
- cotangent: bfloat16 [256, 8192], P('dp'), may hold values from -6 to 6
- gate_weight: bfloat16 [8192, 28672], P(None, ('dp', 'tensor')), may hold values from -0.0625 to 0.0625
- up_weight: bfloat16 [8192, 28672], P(None, ('dp', 'tensor')), may hold values from -0.0625 to 0.0625
- down_weight: bfloat16 [28672, 8192], P(('dp', 'tensor')), may hold values from -0.03125 to 0.03125
- gate_in_proj: bfloat16 [8192, 64], replicated, may hold values from -0.0625 to 0.0625
- up_in_proj: bfloat16 [8192, 64], replicated, may hold values from -0.0625 to 0.0625
- down_out_proj: bfloat16 [8192, 64], replicated, may hold values from -0.0625 to 0.0625
- gate_out_proj: bfloat16 [28672, 64], P(('dp', 'tensor')), may hold values from -0.03125 to 0.03125
- up_out_proj: bfloat16 [28672, 64], P(('dp', 'tensor')), may hold values from -0.03125 to 0.03125
- down_in_proj: bfloat16 [28672, 64], P(('dp', 'tensor')), may hold values from -0.03125 to 0.03125
- stored_grads: bfloat16 [1024, 12288], P(('dp', 'tensor')), may hold values from -0.0546875 to 0.0546875
- example_ids: int32 [1024], P(('dp', 'tensor')), may hold values from 0 to 255
Outputs:
- doc_grads: bfloat16 [8, 12288], P('dp')
- example_scores: float32 [8, 256], P(None, ('dp', 'tensor'))
Inputs may be any that keep to these rules, and one draw needn't show every extreme that they name: `token_ids`: 0 marks padding, which only fills the end of a document of 32 tokens; each document has 16 or more tokens other than 0.
All inputs are finite; a program needn't handle non-finite values.
Results may differ from a plain program's by a relative error of at most 0.0051.
Values may be sent and summed in bfloat16 or wider, within the bound.
A program may use at most 128 MiB of HBM per device.

v0:
```python
import jax
import jax.numpy as jnp
from jax import lax
from jax.sharding import PartitionSpec as P

LEN = 32
EX_DEV = 8


def through_layer(act_rows, cot_rows, gate_part, up_part, down_part):
    gate_pre = jnp.dot(act_rows, gate_part, preferred_element_type=jnp.float32)
    up_pre = jnp.dot(act_rows, up_part, preferred_element_type=jnp.float32)
    back_pre = lax.dot_general(
        cot_rows, down_part, (((1,), (1,)), ((), ())), preferred_element_type=jnp.float32
    )
    return (gate_pre, up_pre, back_pre)


def project_rows(gate_pre, up_pre, back_pre, gate_out_proj, up_out_proj, down_in_proj):
    squash = jax.nn.sigmoid(gate_pre)
    hidden = (gate_pre * squash * up_pre).astype(jnp.bfloat16)
    grad_up = (back_pre * gate_pre * squash).astype(jnp.bfloat16)
    grad_gate = (back_pre * up_pre * squash * (1.0 + gate_pre * (1.0 - squash))).astype(
        jnp.bfloat16
    )
    side_gate = jnp.dot(grad_gate, gate_out_proj, preferred_element_type=jnp.float32)
    side_up = jnp.dot(grad_up, up_out_proj, preferred_element_type=jnp.float32)
    side_down = jnp.dot(hidden, down_in_proj, preferred_element_type=jnp.float32)
    return jnp.concatenate([side_gate, side_up, side_down], axis=1)


def body(
    token_ids,
    hidden_in,
    cotangent,
    gate_weight,
    up_weight,
    down_weight,
    gate_in_proj,
    up_in_proj,
    down_out_proj,
    gate_out_proj,
    up_out_proj,
    down_in_proj,
    stored_grads,
    example_ids,
):
    tok_rows = hidden_in.shape[0]
    proj_rank = gate_in_proj.shape[1]
    pad_mask = (token_ids != 0).astype(jnp.bfloat16)[:, None]
    masked = cotangent * pad_mask
    act_rows = lax.all_gather(hidden_in, "dp", axis=0, tiled=True)
    cot_rows = lax.all_gather(masked, "dp", axis=0, tiled=True)
    gate_pre, up_pre, back_pre = through_layer(
        act_rows, cot_rows, gate_weight, up_weight, down_weight
    )
    block = project_rows(gate_pre, up_pre, back_pre, gate_out_proj, up_out_proj, down_in_proj)
    summed = lax.psum(block, ("dp", "tensor"))
    home_rows = lax.dynamic_slice_in_dim(summed, lax.axis_index("dp") * tok_rows, tok_rows, 0)
    in_gate = jnp.dot(hidden_in, gate_in_proj, preferred_element_type=jnp.float32)
    in_up = jnp.dot(hidden_in, up_in_proj, preferred_element_type=jnp.float32)
    out_down = jnp.dot(masked, down_out_proj, preferred_element_type=jnp.float32)
    docs_here = tok_rows // LEN

    def doc_outer(left, right):
        left_docs = left.reshape(docs_here, LEN, proj_rank)
        right_docs = right.reshape(docs_here, LEN, proj_rank)
        return jnp.einsum("dlr,dls->drs", left_docs, right_docs, precision=lax.Precision.HIGHEST)

    side_gate = home_rows[:, :proj_rank]
    side_up = home_rows[:, proj_rank : 2 * proj_rank]
    side_down = home_rows[:, 2 * proj_rank :]
    blocks = jnp.stack(
        [doc_outer(in_gate, side_gate), doc_outer(in_up, side_up), doc_outer(side_down, out_down)],
        axis=1,
    )
    doc_grads = blocks.reshape(docs_here, 3 * proj_rank * proj_rank).astype(jnp.bfloat16)
    examples_all = EX_DEV * lax.axis_size("dp") * lax.axis_size("tensor")
    onehot = (example_ids[:, None] == jnp.arange(examples_all, dtype=jnp.int32)[None, :]).astype(
        jnp.float32
    )
    raw_scores = lax.dot_general(
        lax.all_gather(doc_grads, "dp", axis=0, tiled=True),
        stored_grads,
        (((1,), (1,)), ((), ())),
        preferred_element_type=jnp.float32,
    )
    partial_scores = jnp.dot(raw_scores, onehot, precision=lax.Precision.HIGHEST)
    totals = lax.psum_scatter(partial_scores, ("dp", "tensor"), scatter_dimension=1, tiled=True)
    return (doc_grads, totals)


def solution(mesh):
    return jax.shard_map(
        body,
        mesh=mesh,
        in_specs=(
            P("dp"),
            P("dp", None),
            P("dp", None),
            P(None, ("dp", "tensor")),
            P(None, ("dp", "tensor")),
            P(("dp", "tensor"), None),
            P(),
            P(),
            P(),
            P(("dp", "tensor"), None),
            P(("dp", "tensor"), None),
            P(("dp", "tensor"), None),
            P(("dp", "tensor"), None),
            P(("dp", "tensor")),
        ),
        out_specs=(P("dp", None), P(None, ("dp", "tensor"))),
        check_vma=False,
    )
```

profile of v0, /device:TPU:0, one launch (start us, length us, event | category | flops | bytes accessed | tf_op | source)
XLA Modules:
  0.0 308.6 jit_solution(5818601708125545720)
XLA Ops:
  7.2 0.0 copy-start
  7.2 0.0 all-gather.6.cloned.1.call-start
  7.2 0.7 all-gather.6.cloned.1.call-update
  7.9 0.0 all-gather.4.cloned.1.call-start
  8.0 0.7 compare_convert_fusion
  8.6 2.0 broadcast_multiply_fusion
  10.6 0.0 all-gather.4.cloned.1.call-update
  10.6 0.0 all-reduce.3.cloned.1.call-start
  10.7 0.0 copy-done
  10.7 1.4 fusion.23
  12.1 1.8 fusion.22
  13.9 45.6 %all-gather.6.cloned.1.call-done = bf16[256,8192]{1,0:T(8,128)(2,1)} async-done(((bf16[32,8192]{1,0:T(8,128)(2,1)}), bf16[256,8192]{1,0:T(8,128)(2,1)}) %all-gather.6.cloned.1.call-update) | async-done | bytes 4194320 | tf_op jit(solution)/shard_map/all_gather | solution.py:52
  59.5 12.8 %fusion.20 = f32[256,896]{1,0:T(8,128)S(1)} fusion(bf16[256,8192]{1,0:T(8,128)(2,1)} %all-gather.6.cloned.1.call-done, bf16[8192,896]{1,0:T(8,128)(2,1)} %param.18), kind=kOutput, calls=%fused_computation.33 | convolution fusion | flops 3758096384 | bytes 19791872 | tf_op jit(solution)/shard_map/dot_general | solution.py:12
  72.3 0.0 copy-done.4
  72.3 0.0 copy-start.9
  72.3 0.0 copy-start.5
  72.3 8.3 %fusion.21 = f32[256,896]{1,0:T(8,128)S(1)} fusion(bf16[256,8192]{1,0:T(8,128)(2,1)S(1)} %copy-done.4, bf16[8192,896]{1,0:T(8,128)(2,1)} %param.17), kind=kOutput, calls=%fused_computation.34 | convolution fusion | flops 3758096384 | bytes 19791872 | tf_op jit(solution)/shard_map/dot_general | solution.py:11
  80.6 0.0 copy-done.9
  80.6 0.0 copy-start.11
  80.6 1.0 copy-done.11
  81.6 0.0 copy-done.5
  81.6 0.4 fusion.4
  82.0 0.0 copy-start.1
  82.0 0.0 copy-start.2
  82.0 0.0 copy-start.3
  82.0 0.0 copy-start.8
  82.0 25.0 %all-gather.4.cloned.1.call-done = bf16[256,8192]{1,0:T(8,128)(2,1)} async-done(((bf16[32,8192]{1,0:T(8,128)(2,1)}), bf16[256,8192]{1,0:T(8,128)(2,1)}) %all-gather.4.cloned.1.call-update) | async-done | bytes 4194320 | tf_op jit(solution)/shard_map/all_gather | solution.py:53
  107.0 11.7 %fusion.19 = f32[256,896]{1,0:T(8,128)S(1)} fusion(bf16[256,8192]{1,0:T(8,128)(2,1)} %all-gather.4.cloned.1.call-done, bf16[896,8192]{1,0:T(8,128)(2,1)} %param.19), kind=kOutput, calls=%fused_computation.32 | convolution fusion | flops 3758096384 | bytes 19791872 | tf_op jit(solution)/shard_map/dot_general | solution.py:13
  118.7 0.0 copy-done.6
  118.7 0.0 copy-done.12
  118.7 0.4 fusion.3
  119.2 0.5 fusion.5
  119.7 0.7 pad_maximum_fusion
  120.4 0.0 all-reduce.3.cloned.1.call-update
  120.4 0.0 copy-done.1
  120.4 0.0 copy-done.2
  120.4 0.4 fusion.18
  120.8 121.5 %all-reduce.3.cloned.1.call-done = f32[256,192]{0,1:T(8,128)} async-done(((f32[256,192]{0,1:T(8,128)}), f32[256,192]{0,1:T(8,128)}) %all-reduce.3.cloned.1.call-update) | async-done | bytes 196624 | tf_op jit(solution)/shard_map/psum | solution.py:58
  242.3 1.0 fusion
  243.4 1.0 fusion.2
  244.4 1.0 fusion.1
  245.4 0.7 convert_element_type.29
  246.1 0.1 reshape.44
  246.2 15.6 %all-gather = bf16[8,1,12288]{2,1,0:T(2,128)(2,1)S(1)} all-gather(bf16[1,1,12288]{2,1,0:T(2,128)(2,1)S(1)} %reshape.44), channel_id=1, replica_groups=mesh['dp'=8,'tensor'=4] {'dp'}, dimensions={0}, use_global_device_ids=true | all-gather | bytes 221184 | tf_op jit(solution)/shard_map/all_gather | solution.py:83
  261.8 0.4 fusion.6
  262.3 0.2 fusion.12
  262.5 39.0 %all-reduce = f32[8,256]{1,0:T(8,128)S(1)} all-reduce(f32[8,256]{1,0:T(8,128)S(1)} %fusion.12), channel_id=2, replica_groups=mesh['dp'=8,'tensor'=4] {'dp','tensor'}, use_global_device_ids=true, to_apply=%region_1.0.clone | all-reduce | flops 2048 | bytes 16384
  301.5 0.7 constant_dynamic-slice_fusion
  (10 shorter events, 0.0 us)
Async XLA Ops:
  7.2 3.5 %copy-start = (bf16[8192,64]{0,1:T(8,128)(2,1)S(1)}, bf16[8192,64]{0,1:T(8,128)(2,1)}, u32[]{:S(2)}) copy-start(bf16[8192,64]{0,1:T(8,128)(2,1)} %param.22) | copy-start | bytes 3145732
  7.2 52.3 %all-gather.6.cloned.1.call-start = ((), (), s32[]{:S(2)}) async-start(), calls=%async_computation.1 | async-start | bytes 4718592 | tf_op jit(solution)/shard_map/all_gather | solution.py:52
  7.9 99.1 %all-gather.4.cloned.1.call-start = ((), (), s32[]{:S(2)}) async-start(), calls=%async_computation | async-start | bytes 4718592 | tf_op jit(solution)/shard_map/all_gather | solution.py:53
  10.6 231.7 %all-reduce.3.cloned.1.call-start = ((), (), s32[]{:S(2)}) async-start(), calls=%async_computation.2 | async-start | bytes 393216 | tf_op jit(solution)/shard_map/psum | solution.py:58
  59.5 12.8 %copy-start.4 = (bf16[256,8192]{1,0:T(8,128)(2,1)S(1)}, bf16[256,8192]{1,0:T(8,128)(2,1)}, u32[]{:S(2)}) copy-start(bf16[256,8192]{1,0:T(8,128)(2,1)} %all-gather.6.cloned.1.call-done) | copy-start | bytes 12582916
  72.3 8.3 %copy-start.9 = (f32[256,896]{1,0:T(8,128)}, f32[256,896]{1,0:T(8,128)S(1)}, u32[]{:S(2)}) copy-start(f32[256,896]{1,0:T(8,128)S(1)} %fusion.20) | copy-start | bytes 2752516
  72.3 9.3 %copy-start.5 = (bf16[896,64]{0,1:T(8,128)(2,1)S(1)}, bf16[896,64]{0,1:T(8,128)(2,1)}, u32[]{:S(2)}) copy-start(bf16[896,64]{0,1:T(8,128)(2,1)} %param.25) | copy-start | bytes 344068
  80.6 1.0 copy-start.11
  82.0 38.4 %copy-start.1 = (bf16[32,8192]{1,0:T(8,128)(2,1)S(1)}, bf16[32,8192]{1,0:T(8,128)(2,1)}, u32[]{:S(2)}) copy-start(bf16[32,8192]{1,0:T(8,128)(2,1)} %param.15) | copy-start | bytes 1572868
  82.0 38.4 %copy-start.2 = (bf16[8192,64]{0,1:T(8,128)(2,1)S(1)}, bf16[8192,64]{0,1:T(8,128)(2,1)}, u32[]{:S(2)}) copy-start(bf16[8192,64]{0,1:T(8,128)(2,1)} %param.20) | copy-start | bytes 3145732
  82.0 179.9 %copy-start.3 = (bf16[32,12288]{1,0:T(8,128)(2,1)S(1)}, bf16[32,12288]{1,0:T(8,128)(2,1)}, u32[]{:S(2)}) copy-start(bf16[32,12288]{1,0:T(8,128)(2,1)} %param.26) | copy-start | bytes 2359300
  82.0 180.3 %copy-start.8 = (s32[32]{0:T(128)S(1)}, s32[32]{0:T(128)}, u32[]{:S(2)}) copy-start(s32[32]{0:T(128)} %param.27) | copy-start | bytes 388
  107.0 11.7 %copy-start.6 = (bf16[896,64]{0,1:T(8,128)(2,1)S(1)}, bf16[896,64]{0,1:T(8,128)(2,1)}, u32[]{:S(2)}) copy-start(bf16[896,64]{0,1:T(8,128)(2,1)} %param.24) | copy-start | bytes 344068
  107.0 11.7 %copy-start.12 = (f32[256,896]{1,0:T(8,128)S(1)}, f32[256,896]{1,0:T(8,128)}, u32[]{:S(2)}) copy-start(f32[256,896]{1,0:T(8,128)} %copy-done.11) | copy-start | bytes 2752516
  107.0 12.1 %copy-start.7 = (bf16[896,64]{0,1:T(8,128)(2,1)S(1)}, bf16[896,64]{0,1:T(8,128)(2,1)}, u32[]{:S(2)}) copy-start(bf16[896,64]{0,1:T(8,128)(2,1)} %param.23) | copy-start | bytes 344068
  107.0 12.1 %copy-start.10 = (f32[256,896]{1,0:T(8,128)S(1)}, f32[256,896]{1,0:T(8,128)}, u32[]{:S(2)}) copy-start(f32[256,896]{1,0:T(8,128)} %copy-done.9) | copy-start | bytes 2752516
Sparse Core Ops, SparseCore 0:
  9.6 49.8 all-gather.5
  61.1 45.8 all-gather.3
  120.5 121.7 all-reduce.2
where the time goes:
time: 309 us
  waiting for transfers between devices  193 us (62%)
  blocking collectives  54.6 us (18%)
  matrix products  41.3 us (13%)
  between operations  14 us (5%)
  other arithmetic  3.36 us (1%)
    psum x1, waiting for transfers between devices, body(): summed = lax.psum(block, ('dp', 'tensor'))  122 us
    all_gather x1, waiting for transfers between devices, body(): act_rows = lax.all_gather(hidden_in, 'dp', axis=0, tiled=True)  45.6 us
    unnamed x1, blocking collectives  39 us
    all_gather x1, waiting for transfers between devices, body(): cot_rows = lax.all_gather(masked, 'dp', axis=0, tiled=True)  25 us
    all_gather x1, blocking collectives, body(): lax.all_gather(doc_grads, 'dp', axis=0, tiled=True)  15.6 us
    dot_general x1, matrix products, through_layer(): up_pre = jnp.dot(act_rows, up_part, preferred_element_type=jnp.float32)  12.8 us
    dot_general x1, matrix products, through_layer(): lax.dot_general(cot_rows, down_part, (((1,), (1,)), ((), ())), preferred_...  11.7 us
    dot_general x1, matrix products, through_layer(): gate_pre = jnp.dot(act_rows, gate_part, preferred_element_type=jnp.float32)  8.27 us
  transfers between devices with their start and end apart: 3, of which 3 were waited for; matrix products, arithmetic and copies ran while one was open for 9% of the time, Pallas kernels for 0%

commit v1 on v0

v1 whole, which is shorter than its diff:
```python
import functools

import jax
import jax.numpy as jnp
from jax import lax
from jax.experimental import pallas as pl
from jax.experimental.pallas import tpu as pltpu
from jax.sharding import PartitionSpec as P

EX_DEV = 8
CORES = 2
SUBS = 2
F32 = jnp.float32
BF16 = jnp.bfloat16
HIGH = lax.Precision.HIGHEST


def await_bytes(ref, sem):
    pltpu.make_async_copy(ref, ref, sem).wait()


def kernel(
    dp,
    tp,
    tok_ref,
    ids_ref,
    hid_ref,
    cot_ref,
    gate_ref,
    up_ref,
    down_ref,
    gin_ref,
    uin_ref,
    dout_ref,
    gout_ref,
    uout_ref,
    din_ref,
    stored_ref,
    grads_out,
    scores_out,
    acts,
    cot_tmp,
    w_buf,
    d_buf,
    in_buf,
    out_buf,
    stored_buf,
    acc,
    in_acc,
    sides,
    side_tx,
    side_rx,
    part_tx,
    part_rx,
    g_sq,
    g_all,
    g_f32,
    g_rows,
    ex_tx,
    ex_rx,
    load_sem,
    w_sem,
    d_sem,
    z_send,
    z_recv,
    p_send,
    p_recv,
    c_send,
    c_recv,
    t_send,
    t_recv,
):
    outer = dp // CORES
    devices = dp * tp
    rows = hid_ref.shape[0]
    width = acts.shape[-1]
    rank = gin_ref.shape[1]
    phases = 2 * SUBS
    d = lax.axis_index("dp")
    t = lax.axis_index("tensor")
    o = d // CORES
    c = d % CORES
    me = d * tp + t
    own = c * outer + o

    def send(src, dst, send_sem, recv_sem, to_d, to_t):
        pltpu.make_async_remote_copy(
            src_ref=src,
            dst_ref=dst,
            send_sem=send_sem,
            recv_sem=recv_sem,
            device_id=(to_d, to_t),
            device_id_type=pl.DeviceIdType.MESH,
        ).start()

    def cols(sub, part):
        return pl.ds(pl.multiple_of((sub * tp + part) * width, width), width)

    cot_load = pltpu.make_async_copy(cot_ref, cot_tmp, load_sem.at[0])
    cot_load.start()
    for sub in range(SUBS):
        for part in range(tp):
            pltpu.make_async_copy(
                hid_ref.at[:, cols(sub, part)], acts.at[sub, part, c, o], load_sem.at[1]
            ).start()

    def weight_loads(sub, part):
        return [
            pltpu.make_async_copy(
                ref.at[cols(sub, part), :], w_buf.at[k, part], w_sem.at[k, part]
            )
            for k, ref in enumerate((gate_ref, up_ref))
        ]

    def down_load(sub, part):
        return pltpu.make_async_copy(
            down_ref.at[:, cols(sub, part)], d_buf.at[sub * tp + part], d_sem.at[sub * tp + part]
        )

    barrier = pltpu.get_barrier_semaphore()

    def greet(k, carry):
        other = (me + k) % devices
        pl.semaphore_signal(
            barrier,
            inc=1,
            device_id=(other // tp, other % tp),
            device_id_type=pl.DeviceIdType.MESH,
        )
        return carry

    lax.fori_loop(1, devices, greet, 0)
    pl.semaphore_wait(barrier, devices - 1)

    def z_sends(p, src):
        for k in range(1, outer):
            to_o = (o + k) % outer
            send(
                src,
                acts.at[p, t, c, o],
                z_send.at[p],
                z_recv.at[p, k],
                to_o * CORES + c,
                t,
            )

    for sub in range(SUBS):
        z_sends(sub, hid_ref.at[:, cols(sub, t)])

    for part in range(tp):
        for load in weight_loads(0, part):
            load.start()
    in_loads = [
        pltpu.make_async_copy(ref, in_buf.at[k], load_sem.at[2 + k])
        for k, ref in enumerate((gin_ref, uin_ref, dout_ref))
    ]
    out_loads = [
        pltpu.make_async_copy(ref, out_buf.at[k], load_sem.at[5 + k])
        for k, ref in enumerate((gout_ref, uout_ref, din_ref))
    ]
    stored_load = pltpu.make_async_copy(stored_ref, stored_buf, load_sem.at[8])
    for load in in_loads:
        load.start()

    cot_load.wait()
    lane = lax.broadcasted_iota(jnp.int32, (rows, rows), 1)
    line = lax.broadcasted_iota(jnp.int32, (rows, rows), 0)
    kept = (tok_ref[...] != 0).astype(F32)
    mask = jnp.sum(jnp.where(lane == line, kept, 0.0), axis=1, keepdims=True)
    for sub in range(SUBS):
        for part in range(tp):
            piece = cot_tmp[:, (sub * tp + part) * width : (sub * tp + part + 1) * width]
            acts[SUBS + sub, part, c, o] = (piece.astype(F32) * mask).astype(BF16)
    for sub in range(SUBS):
        z_sends(SUBS + sub, acts.at[SUBS + sub, t, c, o])
    await_bytes(acts.at[0:SUBS, :, 0, 0], load_sem.at[1])
    for sub in range(SUBS):
        for part in range(tp):
            down_load(sub, part).start()
    for load in out_loads:
        load.start()
    stored_load.start()
    acc[...] = jnp.zeros_like(acc)
    in_acc[...] = jnp.zeros_like(in_acc)

    relay = tp == 4
    if relay:
        x_nb = t + 1 - 2 * (t % 2)
        y_nb = (t + 2) % 4
        first = x_nb + c * (y_nb - x_nb)
        second = y_nb + c * (x_nb - y_nb)
        direct = [first, second]
        diagonal = 3 - t
        others = [first, second, diagonal]
    else:
        direct = [(t + k) % tp for k in range(1, tp)]
        others = [(t + tp - k) % tp for k in range(1, tp)]

    def to_core(p, part):
        send(
            acts.at[p, part, c],
            acts.at[p, part, c],
            c_send.at[p],
            c_recv.at[p],
            o * CORES + 1 - c,
            t,
        )

    def spread(p):
        for k in range(1, outer):
            piece = acts.at[p, t, c, (o + outer - k) % outer]
            await_bytes(piece, z_recv.at[p, k])
            for to_t in direct:
                send(piece, piece, p_send.at[p], p_recv.at[p, t, k], d, to_t)
        to_core(p, t)

    def collect(p):
        for at, part in enumerate(others):
            for k in range(1, outer):
                piece = acts.at[p, part, c, (o + outer - k) % outer]
                await_bytes(piece, p_recv.at[p, part, k])
                if relay and at == 0:
                    send(piece, piece, p_send.at[p], p_recv.at[p, part, k], d, second)
            to_core(p, part)
        await_bytes(acts.at[p, :, 0], c_recv.at[p])

    def forward_part(sub, part):
        for load in weight_loads(sub, part):
            load.wait()
        lhs = acts[sub, part].reshape(dp * rows, width)
        for k in range(2):
            acc[k] += jnp.dot(lhs, w_buf[k, part], preferred_element_type=F32)
            in_acc[k] += jnp.dot(lhs, in_buf[k, cols(sub, part), :], preferred_element_type=F32)
        if sub + 1 < SUBS:
            for load in weight_loads(sub + 1, part):
                load.start()

    def backward_part(sub, part):
        down_load(sub, part).wait()
        lhs = acts[SUBS + sub, part].reshape(dp * rows, width)
        acc[2] += lax.dot_general(
            lhs, d_buf[sub * tp + part], (((1,), (1,)), ((), ())), preferred_element_type=F32
        )
        in_acc[2] += jnp.dot(lhs, in_buf[2, cols(sub, part), :], preferred_element_type=F32)

    def each_part(body):
        def step(part, carry):
            body(part)
            return carry

        lax.fori_loop(0, tp, step, 0)

    def line_block(j):
        return pl.ds(pl.multiple_of(j * rows, rows), rows)

    def gates(j, carry):
        at = line_block(j)
        gate_pre = acc[0, at, :]
        up_pre = acc[1, at, :]
        squash = jax.nn.sigmoid(gate_pre)
        gated = gate_pre * squash
        sides[2, at, :] = (gated * up_pre).astype(BF16)
        acc[0, at, :] = gated
        acc[1, at, :] = up_pre * squash * (1.0 + gate_pre * (1.0 - squash))
        return carry

    def grads(j, carry):
        at = line_block(j)
        back = acc[2, at, :]
        sides[1, at, :] = (back * acc[0, at, :]).astype(BF16)
        sides[0, at, :] = (back * acc[1, at, :]).astype(BF16)
        return carry

    spread(0)
    for p in range(phases):
        if p + 1 < phases:
            spread(p + 1)
        collect(p)
        if p == 0:
            in_loads[0].wait()
            in_loads[1].wait()
        if p == SUBS:
            in_loads[2].wait()
        if p < SUBS:
            each_part(functools.partial(forward_part, p))
        else:
            each_part(functools.partial(backward_part, p - SUBS))
        if p == SUBS - 1:
            lax.fori_loop(0, dp, gates, 0)
            for load in out_loads:
                load.wait()
    lax.fori_loop(0, dp, grads, 0)

    for k in range(3):
        side = jnp.dot(sides[k], out_buf[k], preferred_element_type=F32)
        side_tx[k] = side.astype(BF16).reshape(dp, rows, rank)
        part_tx[k] = side_tx[k, own].astype(F32)

    for k in range(1, dp):
        to_d = (d + k) % dp
        row = (to_d % CORES) * outer + to_d // CORES
        send(
            side_tx.at[:, row], side_rx.at[k], t_send.at[0], t_recv.at[0], to_d, t
        )
    await_bytes(side_rx.at[1:dp], t_recv.at[0])
    for k in range(1, dp):
        part_tx[...] += side_rx[k].astype(F32)
    for k in range(1, tp):
        send(part_tx, part_rx.at[k], t_send.at[1], t_recv.at[1], d, (t + k) % tp)
    await_bytes(part_rx.at[1:tp], t_recv.at[1])
    part_rx[0] = part_tx[...]
    side_sum = jnp.zeros((3, rows, rank), F32)
    for s in range(tp):
        side_sum += part_rx[(t + tp - s) % tp]

    at = line_block(own)
    for k in range(3):
        left, right = in_acc[k, at, :], side_sum[k]
        if k == 2:
            left, right = right, left
        g_sq[k] = lax.dot_general(
            left, right, (((0,), (0,)), ((), ())), precision=HIGH, preferred_element_type=F32
        )
    half = rank // 2
    lines = 3 * half
    for k in range(3):
        even = g_sq[k, pl.ds(0, half, stride=2), :]
        odd = g_sq[k, pl.ds(1, half, stride=2), :]
        g_all[d, k * half : (k + 1) * half, :] = jnp.concatenate([even, odd], axis=1).astype(BF16)
    grads_out[...] = g_all[d]
    for k in range(1, dp):
        send(g_all.at[d], g_all.at[d], t_send.at[2], t_recv.at[2], (d + k) % dp, t)
    stored_load.wait()
    await_bytes(g_all.at[1:dp], t_recv.at[2])
    g_f32[...] = g_all[...].astype(F32)
    for i in range(lines):
        g_rows[:, i * 2 * rank : (i + 1) * 2 * rank] = g_f32[:, i, :]
    raw = lax.dot_general(
        g_rows[...].astype(BF16),
        stored_buf[...],
        (((1,), (1,)), ((), ())),
        preferred_element_type=F32,
    )
    stored_rows = stored_buf.shape[0]
    hot = (
        lax.broadcasted_iota(jnp.int32, (devices * EX_DEV, stored_rows), 0) == ids_ref[...]
    ).astype(F32)
    scattered = lax.dot_general(
        hot, raw, (((1,), (1,)), ((), ())), precision=HIGH, preferred_element_type=F32
    )
    ex_tx[...] = scattered.reshape(devices, EX_DEV, dp)

    def scatter(k, carry):
        other = (me + k) % devices
        send(
            ex_tx.at[other], ex_rx.at[k], t_send.at[3], t_recv.at[3], other // tp, other % tp
        )
        return carry

    lax.fori_loop(1, devices, scatter, 0)
    ex_rx[0] = ex_tx[me]
    await_bytes(ex_rx.at[1:devices], t_recv.at[3])
    scores_out[...] = jnp.sum(ex_rx[...], axis=0)

    for p in range(phases):
        await_bytes(acts.at[p, 0, 0, 1:outer], z_send.at[p])
        await_bytes(acts.at[p, 1:tp, 0, 1:outer], p_send.at[p])
        await_bytes(acts.at[p, :, 0], c_send.at[p])
    await_bytes(side_rx.at[1:dp], t_send.at[0])
    await_bytes(part_rx.at[1:tp], t_send.at[1])
    await_bytes(g_all.at[1:dp], t_send.at[2])
    await_bytes(ex_rx.at[1:devices], t_send.at[3])


def body(dp, tp, *args):
    (
        token_ids,
        hidden_in,
        cotangent,
        gate_weight,
        up_weight,
        down_weight,
        gate_in_proj,
        up_in_proj,
        down_out_proj,
        gate_out_proj,
        up_out_proj,
        down_in_proj,
        stored_grads,
        example_ids,
    ) = args
    rows, model = hidden_in.shape
    hidden_here = gate_weight.shape[1]
    rank = gate_in_proj.shape[1]
    outer = dp // CORES
    devices = dp * tp
    width = model // (tp * SUBS)
    phases = 2 * SUBS
    lines = 3 * rank // 2
    tokens = dp * rows
    dma = pltpu.SemaphoreType.DMA
    vmem = pl.BlockSpec(memory_space=pltpu.VMEM)
    hbm = pl.BlockSpec(memory_space=pl.ANY)
    doc_lines, scores = pl.pallas_call(
        functools.partial(kernel, dp, tp),
        out_shape=(
            jax.ShapeDtypeStruct((lines, 2 * rank), BF16),
            jax.ShapeDtypeStruct((EX_DEV, dp), F32),
        ),
        in_specs=[vmem] * 2 + [hbm] * 12,
        out_specs=(vmem, vmem),
        scratch_shapes=[
            pltpu.VMEM((phases, tp, CORES, outer, rows, width), BF16),
            pltpu.VMEM((rows, model), BF16),
            pltpu.VMEM((2, tp, width, hidden_here), BF16),
            pltpu.VMEM((SUBS * tp, hidden_here, width), BF16),
            pltpu.VMEM((3, model, rank), BF16),
            pltpu.VMEM((3, hidden_here, rank), BF16),
            pltpu.VMEM(stored_grads.shape, BF16),
            pltpu.VMEM((3, tokens, hidden_here), F32),
            pltpu.VMEM((3, tokens, rank), F32),
            pltpu.VMEM((3, tokens, hidden_here), BF16),
            pltpu.VMEM((3, dp, rows, rank), BF16),
            pltpu.VMEM((dp, 3, rows, rank), BF16),
            pltpu.VMEM((3, rows, rank), F32),
            pltpu.VMEM((tp, 3, rows, rank), F32),
            pltpu.VMEM((3, rank, rank), F32),
            pltpu.VMEM((dp, lines, 2 * rank), BF16),
            pltpu.VMEM((dp, lines, 2 * rank), F32),
            pltpu.VMEM((dp, lines * 2 * rank), F32),
            pltpu.VMEM((devices, EX_DEV, dp), F32),
            pltpu.VMEM((devices, EX_DEV, dp), F32),
            dma((9,)),
            dma((2, tp)),
            dma((SUBS * tp,)),
            dma((phases,)),
            dma((phases, outer)),
            dma((phases,)),
            dma((phases, tp, outer)),
            dma((phases,)),
            dma((phases,)),
            dma((4,)),
            dma((4,)),
        ],
        compiler_params=pltpu.CompilerParams(
            collective_id=0, has_side_effects=True, vmem_limit_bytes=60 * 2**20
        ),
    )(
        token_ids.reshape(1, rows),
        example_ids.reshape(1, -1),
        hidden_in,
        cotangent,
        gate_weight,
        up_weight,
        down_weight,
        gate_in_proj,
        up_in_proj,
        down_out_proj,
        gate_out_proj,
        up_out_proj,
        down_in_proj,
        stored_grads,
    )
    return doc_lines.reshape(1, lines * 2 * rank), scores.T


def solution(mesh):
    return jax.shard_map(
        functools.partial(body, mesh.shape["dp"], mesh.shape["tensor"]),
        mesh=mesh,
        in_specs=(
            P("dp"),
            P("dp", None),
            P("dp", None),
            P(None, ("dp", "tensor")),
            P(None, ("dp", "tensor")),
            P(("dp", "tensor"), None),
            P(),
            P(),
            P(),
            P(("dp", "tensor"), None),
            P(("dp", "tensor"), None),
            P(("dp", "tensor"), None),
            P(("dp", "tensor"), None),
            P(("dp", "tensor")),
        ),
        out_specs=(P("dp", None), P(None, ("dp", "tensor"))),
        check_vma=False,
    )
```

time: 309 us -> 118 us (0.38)
  waiting for transfers between devices: 193 us -> 0 us
  Pallas kernels: 0 us -> 101 us
  blocking collectives: 54.6 us -> 0 us
  matrix products: 41.3 us -> 0 us
  local copies, waits for them, and re-layouts: 2.5 us -> 16.2 us
  between operations: 14 us -> 0.64 us
  other arithmetic: 3.36 us -> 0 us
    psum x1 -> x0, waiting for transfers between devices: 122 us -> none  [body(): summed = lax.psum(block, ('dp', 'tensor'))]
    pallas_call x0 -> x1, Pallas kernels: none -> 101 us  [body(): pl.pallas_call(functools.partial(kernel, dp, tp), out_shape=(jax.ShapeDty...]
    all_gather x2 -> x0, waiting for transfers between devices: 70.6 us -> none  [the longest x1 45.6 us: body(): act_rows = lax.all_gather(hidden_in, 'dp', axis=0, tiled=True)]
    dot_general x14 -> x0, matrix products: 41.3 us -> none  [the longest x1 12.8 us: through_layer(): up_pre = jnp.dot(act_rows, up_part, preferred_element_type=jnp.float32)]
    unnamed x1 -> x0, blocking collectives: 39 us -> none
    all_gather x1 -> x0, blocking collectives: 15.6 us -> none  [body(): lax.all_gather(doc_grads, 'dp', axis=0, tiled=True)]
    unnamed x28 -> x8, local copies, waits for them, and re-layouts: 1.79 us -> 16.2 us
  transfers between devices with their start and end apart: 3 -> 0, of which waited for: 3 -> 0; matrix products, arithmetic and copies ran while one was open for 9% -> 0% of each run, Pallas kernels for 0% -> 0%
where the time goes in v1:
time: 118 us
  Pallas kernels  101 us (86%)
  local copies, waits for them, and re-layouts  16.2 us (14%)
    pallas_call x1, Pallas kernels, body(): pl.pallas_call(functools.partial(kernel, dp, tp), out_shape=(jax.ShapeDty...  101 us
    unnamed x8, local copies, waits for them, and re-layouts  16.2 us

profile of v1, /device:TPU:0, one launch (start us, length us, event | category | flops | bytes accessed | tf_op | source)
XLA Modules:
  0.0 117.6 jit_solution(13908029636926948756)
XLA Ops:
  0.6 1.7 %copy.19.gout_ref = bf16[896,64]{1,0:T(8,128)(2,1)} copy(bf16[896,64]{0,1:T(8,128)(2,1)} %param.23) | data formatting | bytes 229376 | tf_op args[9]
  2.4 1.7 %copy.20.uout_ref = bf16[896,64]{1,0:T(8,128)(2,1)} copy(bf16[896,64]{0,1:T(8,128)(2,1)} %param.24) | data formatting | bytes 229376 | tf_op args[10]
  4.1 1.7 %copy.21.din_ref = bf16[896,64]{1,0:T(8,128)(2,1)} copy(bf16[896,64]{0,1:T(8,128)(2,1)} %param.25) | data formatting | bytes 229376 | tf_op args[11]
  5.8 2.8 %copy.16.gin_ref = bf16[8192,64]{1,0:T(8,128)(2,1)} copy(bf16[8192,64]{0,1:T(8,128)(2,1)} %param.20) | data formatting | bytes 2097152 | tf_op args[6]
  8.6 2.7 %copy.17.uin_ref = bf16[8192,64]{1,0:T(8,128)(2,1)} copy(bf16[8192,64]{0,1:T(8,128)(2,1)} %param.21) | data formatting | bytes 2097152 | tf_op args[7]
  11.3 2.8 %copy.18.dout_ref = bf16[8192,64]{1,0:T(8,128)(2,1)} copy(bf16[8192,64]{0,1:T(8,128)(2,1)} %param.22) | data formatting | bytes 2097152 | tf_op args[8]
  14.1 100.7 %shard_map.149 = (bf16[96,128]{1,0:T(8,128)(2,1)}, f32[8,8]{1,0:T(8,128)}) custom-call(s32[1,32]{1,0:T(1,128)} %bitcast.11, s32[1,32]{1,0:T(1,128)} %bitcast.12, bf16[32,8192]{1,0:T(8,128)(2,1)} %hid_ref.1, bf16[32,8192]{1,0:T(8,128)(2,1)} %cot_ref.1, bf16[8192,896]{1,0:T(8,128)(2,1)} %gate_ref.1, bf16[8192,896]{1,0:T(8,128)(2,1)} %up_ref.1, ...), custom_call_target="tpu_custom_call" | custom-call | tf_op jit(solution)/shard_map/pallas_call | solution.py:404
  114.8 1.3 %copy.22 = f32[8,8]{1,0:T(8,128)} copy(f32[8,8]{0,1:T(8,128)} %bitcast.10) | data formatting | bytes 512
  116.2 1.4 %copy.25 = bf16[1,1,96,128]{3,1,2,0:T(2,128)(2,1)} copy(bf16[1,1,96,128]{3,2,1,0:T(8,128)(2,1)} %bitcast.9) | data formatting | bytes 49152
